TPU v7x, 32 devices: a whole 2x2x4 slice. The times are simulated.
32 devices in a mesh: grp: 2 (over x), gz: 16 (over z, y, core).
Axes of the slice: x: 2, y: 2, z: 4, core: 2. Of those that a mesh axis runs over, the one named last changes fastest.
Arguments:
- spectra: float32 [2048, 4096], P(('grp', 'gz')), parts along dimension 0, may hold values from -6 to 6
- offsets: int32 [2048], P(('grp', 'gz')), parts along dimension 0, may hold values from 0 to 8192, as said below
- mask_bits: int32 [2048, 256], P(('grp', 'gz')), parts along dimension 0, may hold values from 0 to 65535
- eigen: float32 [16, 12288], P(None, 'gz'), as said below
- plan: int32 [16, 3], P('grp'), parts along dimension 0, may hold values from 0 to 15, as said below
Outputs:
- coefficients: float32 [32, 5, 256], P(('grp', 'gz')), parts along dimension 0
- eigen_new: float32 [32, 12288], P('grp', 'gz'), parts along dimension 0
There are 2 independent parts, one for each index of `grp`. A program takes and returns all parts, laid end to end along the dimension named above; an argument that names none is the same for every part. Nothing has to cross between parts.
Inputs may be any that keep to these rules, and one draw needn't show every extreme that they name: `offsets`: offset of spectrum g lies between g * 8064 // 1024 and that plus 128; the first spectrum's offset is 0 and the last one's 12288 - 4096. `plan`: row j names devices j and j + 8 (one as source, the other as destination, in either order) and then a block number below 4. `eigen`: rows of the eigenspectra have scales that vary over the pixels.
All inputs are finite; a program needn't handle non-finite values.
Results may differ from a plain program's by a relative error of at most 0.0003.
Values sent between devices are 32-bit elements; how exact they have to be, the bound alone decides.
A program may use at most 64 MiB of HBM per device.

v0:
```python
import math

import jax
import jax.numpy as jnp
from jax import lax
from jax.sharding import PartitionSpec as P

NB = 4
BS = 16
SPAN = 128


def swapped(array, axis, stride):
    return lax.ppermute(array, axis, [(i, i ^ 1 << stride) for i in range(lax.axis_size(axis))])


def unpack_bits(words):
    shifts = jnp.arange(16, dtype=jnp.int32)
    bits = jnp.right_shift(words[..., None], shifts) & 1
    return bits.reshape(words.shape[0], -1).astype(jnp.float32)


def place_rows(rows, shifts, length):

    def place_one(row, start):
        return lax.dynamic_update_slice(jnp.zeros((length,), rows.dtype), row, (start,))

    return jax.vmap(place_one)(rows, shifts)


def take_rows(rows, shifts, width):

    def take_one(row, start):
        return lax.dynamic_slice(row, (start,), (width,))

    return jax.vmap(take_one)(rows, shifts)


def process_block(table, flux, starts, words, length):
    width = flux.shape[1]
    pixels = table.shape[1]
    scale = 1.0 / math.sqrt(width)
    starts = starts.astype(jnp.int32)
    first = jnp.clip(jnp.min(starts), 0, pixels - length)
    window = lax.dynamic_slice_in_dim(table, first, length, 1)
    shifted = starts - first
    goodness = unpack_bits(words)
    masked = place_rows(goodness * flux, shifted, length)
    coef = jnp.dot(masked, window.T, precision=lax.Precision.HIGHEST) * scale
    fitted_window = jnp.dot(coef, window, precision=lax.Precision.HIGHEST) * scale
    fitted = take_rows(fitted_window, shifted, width)
    resid = goodness * (flux - fitted)
    weighted = resid / (1.0 + resid * resid)
    placed = place_rows(weighted, shifted, length)
    grad_window = jnp.dot(coef.T, placed, precision=lax.Precision.HIGHEST)
    return (coef, first, grad_window)


def accumulate(total, first, grad_window):
    length = grad_window.shape[1]
    current = lax.dynamic_slice_in_dim(total, first, length, 1)
    return lax.dynamic_update_slice_in_dim(total, current + grad_window, first, 1)


def local(spectra, offsets, mask_bits, eigen, plan):
    width = spectra.shape[1]
    rank = eigen.shape[0]
    devices = lax.axis_size("gz")
    me_index = lax.axis_index("gz")
    half = plan.shape[0]
    partner_bit = devices.bit_length() - 2
    whole_table = lax.all_gather(eigen, "gz", axis=1, tiled=True)
    pixels = whole_table.shape[1]
    length = min(pixels, width + SPAN + (pixels - width - SPAN) // (NB * devices) + 4)
    plan_row = lax.dynamic_index_in_dim(plan, me_index % half, 0, keepdims=False)
    is_source = plan_row[0] == me_index
    block_id = plan_row[2]
    flux = spectra.reshape(NB, BS, width)
    starts = offsets.reshape(NB, BS)
    words = mask_bits.reshape(NB, BS, width // 16)
    own_block = jnp.arange(NB, dtype=jnp.int32) == block_id
    grad = jnp.zeros((rank, pixels), jnp.float32)
    sent_flux = lax.dynamic_index_in_dim(flux, block_id, 0, keepdims=True)
    sent_starts = lax.dynamic_index_in_dim(starts, block_id, 0, keepdims=True)
    sent_words = lax.dynamic_index_in_dim(words, block_id, 0, keepdims=True)
    got_flux, got_starts, got_words = swapped(
        (sent_flux, sent_starts, sent_words), "gz", partner_bit
    )
    own_valid = jnp.where(is_source & own_block, 0.0, 1.0).astype(jnp.float32)
    extra_valid = jnp.where(is_source, 0.0, 1.0).astype(jnp.float32)
    valid = jnp.concatenate([own_valid, extra_valid[None]])
    all_flux = jnp.concatenate([flux, got_flux], axis=0)
    all_starts = jnp.concatenate([starts, got_starts], axis=0)
    all_words = jnp.concatenate([words, got_words], axis=0)
    coef_list = []
    for block in range(NB + 1):
        coef, first, grad_window = process_block(
            whole_table, all_flux[block], all_starts[block], all_words[block], length
        )
        grad = accumulate(grad, first, grad_window * valid[block])
        coef_list.append((coef * valid[block]).reshape(1, BS * rank))
    coef_out = jnp.concatenate(coef_list, axis=0)
    eta = 2.0 / math.sqrt(devices * spectra.shape[0] * width / pixels)
    grad_mine = lax.psum_scatter(grad, "gz", scatter_dimension=1, tiled=True)
    update = eigen + eta * grad_mine
    squares = lax.psum(jnp.sum(update * update, axis=1), "gz")
    eigen_new = update / jnp.sqrt(squares[:, None] / pixels + 1e-06)
    return (coef_out.reshape(1, NB + 1, BS * rank), eigen_new)


def solution(mesh):
    placed = (
        P(("grp", "gz"), None),
        P(("grp", "gz")),
        P(("grp", "gz"), None),
        P(None, "gz"),
        P("grp", None),
    )
    return jax.shard_map(
        local,
        mesh=mesh,
        in_specs=placed,
        out_specs=(P(("grp", "gz"), None, None), P("grp", "gz")),
        check_vma=False,
    )
```

profile of v0, /device:TPU:0, one launch (start us, length us, event | category | flops | bytes accessed | tf_op | source)
XLA Modules:
  0.0 1671.0 jit_solution(9798048839701420836)
XLA Ops:
  11.8 4.0 collective-permute-start.1
  26.8 21.8 %all_gather.3 = f32[16,12288]{1,0:T(8,128)S(1)} all-gather(f32[16,768]{1,0:T(8,128)} %param.8), channel_id=1, replica_groups=mesh['grp'=2,'gz'=16] {'gz'}, dimensions={1}, use_global_device_ids=true | all-gather | bytes 835584 | tf_op jit(solution)/shard_map/all_gather | solution.py:72
  68.8 125.3 %while.24 = (s32[]{:T(128)}, f32[16,4354]{1,0:T(8,128)S(1)}, s32[16,2]{0,1:T(2,128)S(1)}, f32[16,4096]{1,0:T(8,128)}, s32[]{:T(128)}, /*index=5*/s32[2]{0:T(128)S(1)}) while((s32[]{:T(128)}, f32[16,4354]{1,0:T(8,128)S(1)}, s32[16,2]{0,1:T(2,128)S(1)}, f32[16,4096]{1,0:T(8,128)}, s32[]{:T(128)}, /*index=5*/s32[2]{0:T(128)S(1)}) %tuple.306), condition=%wide.while_cond.9, body=%wide.while_body.9.sunk | while | flops 4107 | bytes 82059 | solution.py:26
  196.0 52.8 %while.19 = (s32[]{:T(128)}, f32[16,4354]{1,0:T(8,128)}, s32[16,2]{0,1:T(2,128)S(1)}, f32[16,4096]{1,0:T(8,128)S(1)}, s32[]{:T(128)}, /*index=5*/s32[]{:T(128)}) while((s32[]{:T(128)}, f32[16,4354]{1,0:T(8,128)}, s32[16,2]{0,1:T(2,128)S(1)}, f32[16,4096]{1,0:T(8,128)S(1)}, s32[]{:T(128)}, /*index=5*/s32[]{:T(128)}) %tuple.262), condition=%wide.while_cond.4, body=%wide.while_body.4.sunk | while | flops 2 | bytes 65649 | solution.py:34
  250.9 129.0 %while.23 = (s32[]{:T(128)}, f32[16,4354]{1,0:T(8,128)S(1)}, s32[16,2]{0,1:T(2,128)S(1)}, f32[16,4096]{1,0:T(8,128)}, s32[]{:T(128)}, /*index=5*/s32[2]{0:T(128)S(1)}) while((s32[]{:T(128)}, f32[16,4354]{1,0:T(8,128)S(1)}, s32[16,2]{0,1:T(2,128)S(1)}, f32[16,4096]{1,0:T(8,128)}, s32[]{:T(128)}, /*index=5*/s32[2]{0:T(128)S(1)}) %tuple.307), condition=%wide.while_cond.8, body=%wide.while_body.8.sunk | while | flops 4107 | bytes 82059 | solution.py:26
  253.7 3.0 broadcast_select_fusion.23
  261.7 3.0 broadcast_select_fusion.23
  269.6 3.0 broadcast_select_fusion.23
  277.6 3.0 broadcast_select_fusion.23
  285.7 3.0 broadcast_select_fusion.23
  381.0 40.5 %while.18 = (s32[]{:T(128)}, f32[16,4354]{1,0:T(8,128)S(1)}, s32[16,2]{0,1:T(2,128)S(1)}, f32[16,4096]{1,0:T(8,128)S(1)}, s32[]{:T(128)}, /*index=5*/s32[]{:T(128)}) while((s32[]{:T(128)}, f32[16,4354]{1,0:T(8,128)S(1)}, s32[16,2]{0,1:T(2,128)S(1)}, f32[16,4096]{1,0:T(8,128)S(1)}, s32[]{:T(128)}, /*index=5*/s32[]{:T(128)}) %tuple.277), condition=%wide.while_cond.3, body=%wide.while_body.3.sunk | while | flops 2 | bytes 65649 | solution.py:34
  421.5 129.0 %while.22 = (s32[]{:T(128)}, f32[16,4354]{1,0:T(8,128)S(1)}, s32[16,2]{0,1:T(2,128)S(1)}, f32[16,4096]{1,0:T(8,128)}, s32[]{:T(128)}, /*index=5*/s32[2]{0:T(128)S(1)}) while((s32[]{:T(128)}, f32[16,4354]{1,0:T(8,128)S(1)}, s32[16,2]{0,1:T(2,128)S(1)}, f32[16,4096]{1,0:T(8,128)}, s32[]{:T(128)}, /*index=5*/s32[2]{0:T(128)S(1)}) %tuple.308), condition=%wide.while_cond.7, body=%wide.while_body.7.sunk | while | flops 4107 | bytes 82059 | solution.py:26
  553.0 52.8 %while.17 = (s32[]{:T(128)}, f32[16,4354]{1,0:T(8,128)}, s32[16,2]{0,1:T(2,128)S(1)}, f32[16,4096]{1,0:T(8,128)S(1)}, s32[]{:T(128)}, /*index=5*/s32[]{:T(128)}) while((s32[]{:T(128)}, f32[16,4354]{1,0:T(8,128)}, s32[16,2]{0,1:T(2,128)S(1)}, f32[16,4096]{1,0:T(8,128)S(1)}, s32[]{:T(128)}, /*index=5*/s32[]{:T(128)}) %tuple.286), condition=%wide.while_cond.2, body=%wide.while_body.2.sunk | while | flops 2 | bytes 65649 | solution.py:34
  606.5 125.0 %while.21 = (s32[]{:T(128)}, f32[16,4354]{1,0:T(8,128)S(1)}, s32[16,2]{0,1:T(2,128)S(1)}, f32[16,4096]{1,0:T(8,128)}, s32[]{:T(128)}, /*index=5*/s32[2]{0:T(128)S(1)}) while((s32[]{:T(128)}, f32[16,4354]{1,0:T(8,128)S(1)}, s32[16,2]{0,1:T(2,128)S(1)}, f32[16,4096]{1,0:T(8,128)}, s32[]{:T(128)}, /*index=5*/s32[2]{0:T(128)S(1)}) %tuple.309), condition=%wide.while_cond.6, body=%wide.while_body.6.sunk | while | flops 4107 | bytes 82059 | solution.py:26
  733.9 53.9 %while.16 = (s32[]{:T(128)}, f32[16,4354]{1,0:T(8,128)}, s32[16,2]{0,1:T(2,128)S(1)}, f32[16,4096]{1,0:T(8,128)S(1)}, s32[]{:T(128)}, /*index=5*/s32[]{:T(128)}) while((s32[]{:T(128)}, f32[16,4354]{1,0:T(8,128)}, s32[16,2]{0,1:T(2,128)S(1)}, f32[16,4096]{1,0:T(8,128)S(1)}, s32[]{:T(128)}, /*index=5*/s32[]{:T(128)}) %tuple.283), condition=%wide.while_cond.1, body=%wide.while_body.1.sunk | while | flops 2 | bytes 65649 | solution.py:34
  788.6 126.4 %while.20 = (s32[]{:T(128)}, f32[16,4354]{1,0:T(8,128)S(1)}, s32[16,2]{0,1:T(2,128)S(1)}, f32[16,4096]{1,0:T(8,128)}, s32[]{:T(128)}, /*index=5*/s32[2]{0:T(128)S(1)}) while((s32[]{:T(128)}, f32[16,4354]{1,0:T(8,128)S(1)}, s32[16,2]{0,1:T(2,128)S(1)}, f32[16,4096]{1,0:T(8,128)}, s32[]{:T(128)}, /*index=5*/s32[2]{0:T(128)S(1)}) %tuple.310), condition=%wide.while_cond.5, body=%wide.while_body.5.sunk | while | flops 4107 | bytes 82059 | solution.py:26
  916.7 39.4 %while.15 = (s32[]{:T(128)}, f32[16,4354]{1,0:T(8,128)S(1)}, s32[16,2]{0,1:T(2,128)S(1)}, f32[16,4096]{1,0:T(8,128)S(1)}, s32[]{:T(128)}, /*index=5*/s32[]{:T(128)}) while((s32[]{:T(128)}, f32[16,4354]{1,0:T(8,128)S(1)}, s32[16,2]{0,1:T(2,128)S(1)}, f32[16,4096]{1,0:T(8,128)S(1)}, s32[]{:T(128)}, /*index=5*/s32[]{:T(128)}) %tuple.280), condition=%wide.while_cond, body=%wide.while_body.sunk | while | flops 2 | bytes 65649 | solution.py:34
  958.3 114.5 %while.25 = (s32[]{:T(128)}, f32[16,4354]{1,0:T(8,128)S(1)}, s32[16,2]{0,1:T(2,128)S(1)}, f32[16,4096]{1,0:T(8,128)S(1)}, s32[]{:T(128)}, /*index=5*/s32[2]{0:T(128)S(1)}) while((s32[]{:T(128)}, f32[16,4354]{1,0:T(8,128)S(1)}, s32[16,2]{0,1:T(2,128)S(1)}, f32[16,4096]{1,0:T(8,128)S(1)}, s32[]{:T(128)}, /*index=5*/s32[2]{0:T(128)S(1)}) %tuple.320), condition=%wide.while_cond.10, body=%wide.while_body.10.sunk | while | flops 4107 | bytes 82059 | solution.py:26
  1073.8 129.0 %while.26 = (s32[]{:T(128)}, f32[16,4354]{1,0:T(8,128)S(1)}, s32[16,2]{0,1:T(2,128)S(1)}, f32[16,4096]{1,0:T(8,128)}, s32[]{:T(128)}, /*index=5*/s32[2]{0:T(128)S(1)}) while((s32[]{:T(128)}, f32[16,4354]{1,0:T(8,128)S(1)}, s32[16,2]{0,1:T(2,128)S(1)}, f32[16,4096]{1,0:T(8,128)}, s32[]{:T(128)}, /*index=5*/s32[2]{0:T(128)S(1)}) %tuple.319), condition=%wide.while_cond.11, body=%wide.while_body.11.sunk | while | flops 4107 | bytes 82059 | solution.py:26
  1205.3 126.6 %while.27 = (s32[]{:T(128)}, f32[16,4354]{1,0:T(8,128)S(1)}, s32[16,2]{0,1:T(2,128)S(1)}, f32[16,4096]{1,0:T(8,128)}, s32[]{:T(128)}, /*index=5*/s32[2]{0:T(128)S(1)}) while((s32[]{:T(128)}, f32[16,4354]{1,0:T(8,128)S(1)}, s32[16,2]{0,1:T(2,128)S(1)}, f32[16,4096]{1,0:T(8,128)}, s32[]{:T(128)}, /*index=5*/s32[2]{0:T(128)S(1)}) %tuple.318), condition=%wide.while_cond.12, body=%wide.while_body.12.sunk | while | flops 4107 | bytes 82059 | solution.py:26
  1334.0 111.9 %while.28 = (s32[]{:T(128)}, f32[16,4354]{1,0:T(8,128)S(1)}, s32[16,2]{0,1:T(2,128)S(1)}, f32[16,4096]{1,0:T(8,128)S(1)}, s32[]{:T(128)}, /*index=5*/s32[2]{0:T(128)S(1)}) while((s32[]{:T(128)}, f32[16,4354]{1,0:T(8,128)S(1)}, s32[16,2]{0,1:T(2,128)S(1)}, f32[16,4096]{1,0:T(8,128)S(1)}, s32[]{:T(128)}, /*index=5*/s32[2]{0:T(128)S(1)}) %tuple.317), condition=%wide.while_cond.13, body=%wide.while_body.13.sunk | while | flops 4107 | bytes 82059 | solution.py:26
  1447.9 126.4 %while.29 = (s32[]{:T(128)}, f32[16,4354]{1,0:T(8,128)S(1)}, s32[16,2]{0,1:T(2,128)S(1)}, f32[16,4096]{1,0:T(8,128)}, s32[]{:T(128)}, /*index=5*/s32[2]{0:T(128)S(1)}) while((s32[]{:T(128)}, f32[16,4354]{1,0:T(8,128)S(1)}, s32[16,2]{0,1:T(2,128)S(1)}, f32[16,4096]{1,0:T(8,128)}, s32[]{:T(128)}, /*index=5*/s32[2]{0:T(128)S(1)}) %tuple.316), condition=%wide.while_cond.14, body=%wide.while_body.14.sunk | while | flops 4107 | bytes 82059 | solution.py:26
  1577.6 53.9 %reduce-scatter.2.cloned.1.call-done = f32[16,768]{1,0:T(8,128)} async-done(((f32[16,12288]{1,0:T(8,128)}), f32[16,768]{1,0:T(8,128)}) %reduce-scatter.2.cloned.1.call-update) | async-done | bytes 49168 | tf_op jit(solution)/shard_map/reduce_scatter | solution.py:104
  1633.0 29.6 %psum.7 = f32[16]{0:T(128)S(1)} all-reduce(f32[16]{0:T(128)S(1)} %multiply_reduce_fusion), channel_id=1, replica_groups=mesh['grp'=2,'gz'=16] {'gz'}, use_global_device_ids=true, to_apply=%region_17.18 | all-reduce | flops 16 | bytes 128 | tf_op jit(solution)/shard_map/psum | solution.py:106
  (1228 shorter events, 1516.0 us)
Async XLA Ops:
  7.2 0.7 copy-start
  7.2 1624.3 %reduce-scatter.2.cloned.1.call-start = ((), (), s32[]{:S(2)}) async-start(), calls=%async_computation.1 | async-start | bytes 835584 | tf_op jit(solution)/shard_map/reduce_scatter | solution.py:104
  11.8 52.2 %collective-permute-start.1 = (s32[1,16,256]{2,1,0:T(8,128)}, s32[1,16,256]{2,1,0:T(8,128)S(1)}, u32[]{:S(2)}, u32[]{:S(2)}) collective-permute-start(s32[1,16,256]{2,1,0:T(8,128)} %constant_dynamic-slice_fusion.16), channel_id=1, source_target_pairs={{0,8},{1,9},{2,10},{3,11},{4,12},{5,13},{6,14},{7,15},{8,0},{9,1},... | collective-permute-start | bytes 49160 | tf_op jit(solution)/shard_map/ppermute | solution.py:14
  17.5 49.4 %collective-permute-start.2 = (f32[1,16,4096]{2,1,0:T(8,128)}, f32[1,16,4096]{2,1,0:T(8,128)}, u32[]{:S(2)}, u32[]{:S(2)}) collective-permute-start(f32[1,16,4096]{2,1,0:T(8,128)} %constant_dynamic-slice_fusion.15), channel_id=1, source_target_pairs={{0,8},{1,9},{2,10},{3,11},{4,12},{5,13},{6,14},{7,15},{8,0},{9,1},... | collective-permute-start | bytes 786440 | tf_op jit(solution)/shard_map/ppermute | solution.py:14
  18.2 44.4 %collective-permute-start = (s32[1,16]{1,0:T(1,128)S(1)}, s32[1,16]{1,0:T(1,128)S(1)}, u32[]{:S(2)}, u32[]{:S(2)}) collective-permute-start(s32[1,16]{1,0:T(1,128)S(1)} %constant_dynamic-slice_fusion.17), channel_id=1, source_target_pairs={{0,8},{1,9},{2,10},{3,11},{4,12},{5,13},{6,14},{7,15},{8,0},{9,1},... | collective-permute-start | bytes 200 | tf_op jit(solution)/shard_map/ppermute | solution.py:14
  55.8 6.1 copy-start.10
  64.6 4.2 copy-start.6
  66.9 181.9 %copy-start.2 = (f32[64,4096]{1,0:T(8,128)S(1)}, f32[64,4096]{1,0:T(8,128)}, u32[]{:S(2)}) copy-start(f32[64,4096]{1,0:T(8,128)} %param.5) | copy-start | bytes 3145732
  66.9 181.9 %copy-start.3 = (s32[16,4096]{1,0:T(8,128)S(1)}, s32[16,4096]{1,0:T(8,128)}, u32[]{:S(2)}) copy-start(s32[16,4096]{1,0:T(8,128)} %shift_right_arithmetic.112) | copy-start | bytes 786436
  66.9 181.9 %copy-start.4 = (s32[16,4096]{1,0:T(8,128)S(1)}, s32[16,4096]{1,0:T(8,128)}, u32[]{:S(2)}) copy-start(s32[16,4096]{1,0:T(8,128)} %shift_right_arithmetic.115) | copy-start | bytes 786436
  66.9 181.9 %copy-start.5 = (s32[16,4096]{1,0:T(8,128)S(1)}, s32[16,4096]{1,0:T(8,128)}, u32[]{:S(2)}) copy-start(s32[16,4096]{1,0:T(8,128)} %shift_right_arithmetic.119) | copy-start | bytes 786436
  605.7 0.7 copy-start.7
  787.9 0.7 copy-start.8
  1445.9 131.3 %copy-start.11 = (f32[16,16]{1,0:T(8,128)S(1)}, f32[16,16]{1,0:T(8,128)}, u32[]{:S(2)}) copy-start(f32[16,16]{1,0:T(8,128)} %get-tuple-element.325) | copy-start | bytes 3076
  1445.9 131.4 %copy-start.12 = (f32[16,16]{1,0:T(8,128)S(1)}, f32[16,16]{1,0:T(8,128)}, u32[]{:S(2)}) copy-start(f32[16,16]{1,0:T(8,128)} %get-tuple-element.323) | copy-start | bytes 3076
  1447.0 130.4 %copy-start.13 = (f32[16,16]{1,0:T(8,128)S(1)}, f32[16,16]{1,0:T(8,128)}, u32[]{:S(2)}) copy-start(f32[16,16]{1,0:T(8,128)} %get-tuple-element.321) | copy-start | bytes 3076
  1447.0 184.4 %copy-start.9 = (f32[16,768]{1,0:T(8,128)S(1)}, f32[16,768]{1,0:T(8,128)}, u32[]{:S(2)}) copy-start(f32[16,768]{1,0:T(8,128)} %param.8) | copy-start | bytes 147460
  1576.2 0.9 copy-start.1
Sparse Core Ops, SparseCore 0:
  1577.3 54.1 reduce-scatter.1
where the time goes:
time: 1690 us; the launch traced here: 1670 us
  other arithmetic  779 us (46%)
  local copies, waits for them, and re-layouts  734 us (43%)
  waiting for transfers between devices  53.9 us (3%)
  blocking collectives  51.4 us (3%)
  between operations  22.8 us (1%)
    scatter x320, other arithmetic  768 us
    scatter x480, local copies, waits for them, and re-layouts  470 us
    gather x320, local copies, waits for them, and re-layouts  237 us
    reduce_scatter x1, waiting for transfers between devices, local(): grad_mine = lax.psum_scatter(grad, 'gz', scatter_dimension=1, tiled=True)  53.9 us
  transfers between devices with their start and end apart: 4, of which 1 were waited for; matrix products, arithmetic and copies ran while one was open for 1% of the time, Pallas kernels for 0%

commit v1 on v0

v1 whole, which is shorter than its diff:
```python
import functools
import math

import jax
import jax.numpy as jnp
from jax import lax
from jax.experimental import pallas as pl
from jax.experimental.pallas import tpu as pltpu
from jax.sharding import PartitionSpec as P

NB = 4
BS = 16
SPAN = 128
LANES = 128
TILE = 256


class Geometry:
    def __init__(self, devices, rows, width, pixels, rank):
        self.devices, self.rows, self.width = devices, rows, width
        self.pixels, self.rank = pixels, rank
        self.total = devices * rows
        self.ramp = pixels - width - SPAN
        per_block = ((BS - 1) * self.ramp) // self.total + 1
        self.reach = -(-(per_block + SPAN + LANES - 1) // LANES)
        self.sub = width // LANES + self.reach
        lead = (((NB - 1) * BS * self.ramp) // self.total + LANES) // LANES
        win = self.sub + lead
        self.win = win + win % 2
        self.window = self.win * LANES
        self.scale = 1.0 / math.sqrt(width)
        self.eta = 2.0 / math.sqrt(self.total * width / pixels)

    def aligned(self, spectrum, chunks):
        start = lax.div(lax.div(spectrum * self.ramp, self.total), LANES)
        return jnp.minimum(start, self.pixels // LANES - chunks)

    def device_chunk(self, device):
        return self.aligned(device * self.rows, self.win)

    def block_chunk(self, device, block):
        return self.aligned(device * self.rows + block * BS, self.sub)


def split(x):
    high = x.astype(jnp.bfloat16)
    low = (x - high.astype(jnp.float32)).astype(jnp.bfloat16)
    return high, low


def columns(chunk, count=1):
    return pl.ds(pl.multiple_of(chunk * LANES, LANES), count * LANES)


def lane_take(x, index):
    return jnp.take_along_axis(x, index, axis=1, mode="promise_in_bounds")


def place(geo, me, flux_ref, off_ref, word_ref, pf, pm, phl):
    edge = max(geo.win - geo.sub, 1)
    for lo in (0, geo.win - edge):
        cols = pl.ds(lo * LANES, edge * LANES)
        pf[:, cols] = jnp.zeros((geo.rows, edge * LANES), jnp.float32)
        pm[:, cols] = jnp.zeros((geo.rows, edge * LANES), jnp.float32)
        phl[:, cols] = jnp.zeros((2 * geo.rows, edge * LANES), jnp.bfloat16)
    device_chunk = geo.device_chunk(me)
    lane = lax.broadcasted_iota(jnp.int32, (BS, LANES), 1)
    row = lax.broadcasted_iota(jnp.int32, (BS, LANES), 0)
    flux_chunks = geo.width // LANES

    def body(block, carry):
        first = geo.block_chunk(me, block)
        delta = first - device_chunk
        base = pl.multiple_of(block * BS, BS)
        offs = jnp.zeros((BS, LANES), jnp.int32)
        for s in range(BS):
            offs = jnp.where(row == s, off_ref[base + s], offs)
        u = lane - (offs - first * LANES)
        back = lax.shift_right_arithmetic(u, 7)
        lane_index = u & (LANES - 1)
        bit = u & 15
        word = lax.shift_right_arithmetic(u, 4)
        picks = [back == -d for d in range(geo.reach)]
        zero = jnp.zeros((BS, LANES), jnp.float32)
        words = [
            word_ref[pl.ds(base, BS), pl.ds(i * LANES, LANES)]
            for i in range(geo.width // 16 // LANES)
        ]
        per_word = 16 * LANES
        taken = {}
        for c in range(geo.sub):
            if c < flux_chunks:
                taken[c] = lane_take(
                    flux_ref[pl.ds(base, BS), pl.ds(c * LANES, LANES)], lane_index
                )
            value = taken.get(c - geo.reach, zero)
            for d in reversed(range(geo.reach)):
                value = jnp.where(picks[d], taken.get(c - d, zero), value)
            taken.pop(c - geo.reach, None)
            index = (word + 8 * c) & (LANES - 1)
            lowest = max((c - geo.reach) * LANES, 0)
            highest = min(c * LANES + LANES - 1, geo.width - 1)
            first_word, last_word = lowest // per_word, highest // per_word
            bits = lane_take(words[first_word], index)
            for w in range(first_word + 1, last_word + 1):
                later = u >= w * per_word - c * LANES
                bits = jnp.where(later, lane_take(words[w], index), bits)
            bits = lax.shift_right_logical(bits, bit) & 1
            if c < geo.reach:
                bits = jnp.where(u >= -c * LANES, bits, 0)
            if c >= flux_chunks:
                bits = jnp.where(u < geo.width - c * LANES, bits, 0)
            good = bits.astype(jnp.float32)
            value = value * good
            high, low = split(value)
            cols = columns(delta + c)
            pf[pl.ds(base, BS), cols] = value
            pm[pl.ds(base, BS), cols] = good
            phl[pl.ds(base, BS), cols] = high
            phl[pl.ds(geo.rows + base, BS), cols] = low
        return carry

    lax.fori_loop(0, NB, body, 0)


def solve(geo, me, table, pf, pm, phl, est, grad):
    rank, rows = geo.rank, geo.rows
    start = geo.device_chunk(me)
    step = TILE // LANES
    tiles = geo.win // step
    for t in range(tiles):
        high, low = split(table[:, columns(start + t * step, step)])
        cols = pl.ds(t * TILE, TILE)
        est[pl.ds(0, rank), cols] = high
        est[pl.ds(rank, rank), cols] = low
        est[pl.ds(2 * rank, rank), cols] = high
    both = lax.dot_general(
        phl[...],
        est[pl.ds(0, 2 * rank), :],
        (((1,), (1,)), ((), ())),
        preferred_element_type=jnp.float32,
    )
    both = both[:rows] + both[rows:]
    coef = (both[:, :rank] + both[:, rank:]) * geo.scale
    high, low = split(coef * geo.scale)
    high, low = high.astype(jnp.float32), low.astype(jnp.float32)
    left = jnp.concatenate([high, high, low], axis=1).astype(jnp.bfloat16)
    padded = jnp.concatenate([coef, jnp.zeros((rows, LANES - rank), jnp.float32)], axis=1)
    high, low = split(padded.T[:rank])
    high, low = high.astype(jnp.float32), low.astype(jnp.float32)
    across = jnp.concatenate([high, high, low], axis=1).astype(jnp.bfloat16)
    for t in range(tiles):
        cols = pl.ds(t * TILE, TILE)
        fit = jnp.dot(left, est[:, cols], preferred_element_type=jnp.float32)
        resid = pf[:, cols] - pm[:, cols] * fit
        weighted = resid / (1.0 + resid * resid)
        high, low = split(weighted)
        stack = jnp.concatenate([high, low, high], axis=0)
        grad[:, columns(start + t * step, step)] = jnp.dot(
            across, stack, preferred_element_type=jnp.float32
        )
    return coef


def plain_kernel(geo, flux_ref, off_ref, word_ref, table_ref, coef_ref, grad_ref, pf, pm, phl, est):
    me = lax.axis_index("gz")
    grad_ref[...] = jnp.zeros_like(grad_ref)
    place(geo, me, flux_ref, off_ref, word_ref, pf, pm, phl)
    coef_ref[...] = solve(geo, me, table_ref, pf, pm, phl, est, grad_ref)


def window_scratch(geo):
    return [
        pltpu.VMEM((geo.rows, geo.window), jnp.float32),
        pltpu.VMEM((geo.rows, geo.window), jnp.float32),
        pltpu.VMEM((2 * geo.rows, geo.window), jnp.bfloat16),
        pltpu.VMEM((3 * geo.rank, geo.window), jnp.bfloat16),
    ]


def plain(geo, spectra, offsets, mask_bits, eigen, plan):
    me = lax.axis_index("gz")
    table = lax.all_gather(eigen, "gz", axis=1, tiled=True)
    vmem = pl.BlockSpec(memory_space=pltpu.VMEM)
    smem = pl.BlockSpec(memory_space=pltpu.SMEM)
    coef, grad = pl.pallas_call(
        functools.partial(plain_kernel, geo),
        out_shape=(
            jax.ShapeDtypeStruct((geo.rows, geo.rank), jnp.float32),
            jax.ShapeDtypeStruct((geo.rank, geo.pixels), jnp.float32),
        ),
        in_specs=[vmem, smem, vmem, vmem],
        out_specs=(vmem, vmem),
        scratch_shapes=window_scratch(geo),
        compiler_params=pltpu.CompilerParams(vmem_limit_bytes=40 << 20),
    )(spectra, offsets, mask_bits, table)
    half = plan.shape[0]
    row = lax.dynamic_index_in_dim(plan, me % half, 0, keepdims=False)
    source, block = row[0] == me, row[2]
    blocks = coef.reshape(NB, BS * geo.rank)
    sent = lax.dynamic_index_in_dim(blocks, block, 0, keepdims=True)
    pairs = [(i, (i + half) % geo.devices) for i in range(geo.devices)]
    got = lax.ppermute(sent, "gz", pairs)
    own = jnp.arange(NB, dtype=jnp.int32)[:, None] == block
    blocks = jnp.where(source & own, 0.0, blocks)
    got = jnp.where(source, 0.0, got)
    coefficients = jnp.concatenate([blocks, got], axis=0)[None]
    mine = lax.psum_scatter(grad, "gz", scatter_dimension=1, tiled=True)
    update = eigen + geo.eta * mine
    squares = lax.psum(jnp.sum(update * update, axis=1), "gz")
    eigen_new = update / jnp.sqrt(squares[:, None] / geo.pixels + 1e-06)
    return coefficients, eigen_new


def local(spectra, offsets, mask_bits, eigen, plan):
    devices = lax.axis_size("gz")
    rank, shard = eigen.shape
    geo = Geometry(devices, spectra.shape[0], spectra.shape[1], shard * devices, rank)
    return plain(geo, spectra, offsets, mask_bits, eigen, plan)


def solution(mesh):
    placed = (
        P(("grp", "gz"), None),
        P(("grp", "gz")),
        P(("grp", "gz"), None),
        P(None, "gz"),
        P("grp", None),
    )
    return jax.shard_map(
        local,
        mesh=mesh,
        in_specs=placed,
        out_specs=(P(("grp", "gz"), None, None), P("grp", "gz")),
        check_vma=False,
    )
```

time: 1690 us -> 135 us (0.08); the launches traced: 1670 us -> 135 us
  other arithmetic: 779 us -> 2.45 us
  local copies, waits for them, and re-layouts: 734 us -> 2.54 us
    scatter x320 -> x0, other arithmetic: 768 us -> none
    scatter x480 -> x0, local copies, waits for them, and re-layouts: 470 us -> none
    gather x320 -> x0, local copies, waits for them, and re-layouts: 237 us -> none
  transfers between devices with their start and end apart: 4 -> 2, of which waited for: 1 -> 2; matrix products, arithmetic and copies ran while one was open for 1% -> 1% of each run, Pallas kernels for 0% -> 0%
where the time goes in v1:
time: 135 us
  blocking collectives  55.3 us (41%)
  waiting for transfers between devices  49.9 us (37%)
  between operations  16.7 us (12%)
  Pallas kernels  7.55 us (6%)
  local copies, waits for them, and re-layouts  2.54 us (2%)
  other arithmetic  2.45 us (2%)
    reduce_scatter x1, waiting for transfers between devices, plain(): mine = lax.psum_scatter(grad, 'gz', scatter_dimension=1, tiled=True)  46.8 us
    psum x1, blocking collectives, plain(): squares = lax.psum(jnp.sum(update * update, axis=1), 'gz')  29.6 us
    all_gather x1, blocking collectives, plain(): table = lax.all_gather(eigen, 'gz', axis=1, tiled=True)  25.7 us
    pallas_call x1, Pallas kernels, plain(): pl.pallas_call(functools.partial(plain_kernel, geo), out_shape=(jax.Shape...  7.55 us
    ppermute x1, waiting for transfers between devices, plain(): got = lax.ppermute(sent, 'gz', pairs)  3.07 us
  transfers between devices with their start and end apart: 2, of which 2 were waited for; matrix products, arithmetic and copies ran while one was open for 1% of the time, Pallas kernels for 0%

profile of v1, /device:TPU:0, one launch (start us, length us, event | category | flops | bytes accessed | tf_op | source)
XLA Modules:
  0.0 134.5 jit_solution(7402028126466309033)
XLA Ops:
  7.2 0.0 copy-start
  7.2 0.0 copy-start.3
  7.2 0.0 copy-start.2
  7.2 0.0 reduce-scatter.2.cloned.1.call-start
  7.2 25.7 %all_gather.3.table_ref = f32[16,12288]{1,0:T(8,128)S(1)} all-gather(f32[16,768]{1,0:T(8,128)} %param.8), channel_id=1, replica_groups=mesh['grp'=2,'gz'=16] {'gz'}, dimensions={1}, use_global_device_ids=true | all-gather | bytes 835584 | tf_op jit(solution)/shard_map/all_gather | solution.py:183
  33.0 0.0 copy-done.3
  33.0 0.0 copy-done.2
  33.0 1.2 copy-done.1
  34.2 7.5 %shard_map.68 = (f32[64,16]{1,0:T(8,128)S(1)}, f32[16,12288]{1,0:T(8,128)}) custom-call(f32[64,4096]{1,0:T(8,128)S(1)} %copy-done.1, s32[64]{0:T(128)S(1)} %copy-done.3, s32[64,256]{1,0:T(8,128)S(1)} %copy-done.2, f32[16,12288]{1,0:T(8,128)S(1)} %all_gather.3.table_ref), custom_call_target="tpu_custom_call" | custom-call | tf_op jit(solution)/shard_map/pallas_call | solution.py:186
  41.7 0.0 reduce-scatter.2.cloned.1.call-update
  41.8 0.0 copy-start.4
  41.8 0.1 reshape.22
  41.9 0.0 copy-done
  41.9 0.1 constant_dynamic-slice_fusion.1
  42.0 0.5 fusion
  44.4 0.1 collective-permute-start
  45.2 0.7 compare_and_fusion
  45.8 0.1 broadcast_select_fusion
  45.9 3.1 %collective-permute-done = f32[1,256]{1,0:T(1,128)S(1)} collective-permute-done((f32[1,256]{1,0:T(1,128)S(1)}, f32[1,256]{1,0:T(1,128)S(1)}, u32[]{:S(2)}, u32[]{:S(2)}) %collective-permute-start) | collective-permute-done | bytes 1056 | tf_op jit(solution)/shard_map/ppermute | solution.py:203
  49.0 46.8 %reduce-scatter.2.cloned.1.call-done = f32[16,768]{1,0:T(8,128)} async-done(((f32[16,12288]{1,0:T(8,128)}), f32[16,768]{1,0:T(8,128)}) %reduce-scatter.2.cloned.1.call-update) | async-done | bytes 49168 | tf_op jit(solution)/shard_map/reduce_scatter | solution.py:208
  95.8 1.0 multiply_reduce_fusion
  96.8 0.6 copy.7
  97.4 29.6 %psum.7 = f32[16]{0:T(128)S(1)} all-reduce(f32[16]{0:T(128)S(1)} %multiply_reduce_fusion), channel_id=1, replica_groups=mesh['grp'=2,'gz'=16] {'gz'}, use_global_device_ids=true, to_apply=%region_2.3 | all-reduce | flops 16 | bytes 128 | tf_op jit(solution)/shard_map/psum | solution.py:210
  127.0 0.7 broadcast_divide_fusion
  (8 shorter events, 0.0 us)
Async XLA Ops:
  7.2 34.7 %copy-start = (s32[8,3]{0,1:T(4,128)S(1)}, s32[8,3]{0,1:T(4,128)}, u32[]{:S(2)}) copy-start(s32[8,3]{0,1:T(4,128)} %param.9) | copy-start | bytes 292
  7.2 25.8 %copy-start.3 = (s32[64]{0:T(128)S(1)}, s32[64]{0:T(128)}, u32[]{:S(2)}) copy-start(s32[64]{0:T(128)} %off_ref.1) | copy-start | bytes 772
  7.2 25.8 %copy-start.2 = (s32[64,256]{1,0:T(8,128)S(1)}, s32[64,256]{1,0:T(8,128)}, u32[]{:S(2)}) copy-start(s32[64,256]{1,0:T(8,128)} %word_ref.1) | copy-start | bytes 196612
  7.2 88.6 %reduce-scatter.2.cloned.1.call-start = ((), (), s32[]{:S(2)}) async-start(), calls=%async_computation.1 | async-start | bytes 835584 | tf_op jit(solution)/shard_map/reduce_scatter | solution.py:208
  33.0 1.2 copy-start.1
  41.8 54.0 %copy-start.4 = (f32[16,768]{1,0:T(8,128)S(1)}, f32[16,768]{1,0:T(8,128)}, u32[]{:S(2)}) copy-start(f32[16,768]{1,0:T(8,128)} %param.8) | copy-start | bytes 147460
  44.4 4.5 %collective-permute-start = (f32[1,256]{1,0:T(1,128)S(1)}, f32[1,256]{1,0:T(1,128)S(1)}, u32[]{:S(2)}, u32[]{:S(2)}) collective-permute-start(f32[1,256]{1,0:T(1,128)S(1)} %constant_dynamic-slice_fusion), channel_id=1, source_target_pairs={{0,8},{1,9},{2,10},{3,11},{4,12},{5,13},{6,14},{7,15},{8,0},{9,1},... | collective-permute-start | bytes 3080 | tf_op jit(solution)/shard_map/ppermute | solution.py:203
  95.8 31.2 %copy-start.5 = (f32[16,768]{1,0:T(8,128)S(1)}, f32[16,768]{1,0:T(8,128)}, u32[]{:S(2)}) copy-start(f32[16,768]{1,0:T(8,128)} %reduce-scatter.2.cloned.1.call-done) | copy-start | bytes 147460
Sparse Core Ops, SparseCore 0:
  41.9 53.8 reduce-scatter.1

commit v2 on v1

--- a/solution.py
+++ b/solution.py
@@ -212,10 +212,196 @@
     return coefficients, eigen_new
 
 
+def fused_kernel(
+    geo, half, flux_ref, off_ref, word_ref, eigen_ref, plan_ref, coef_ref, new_ref,
+    pf, pm, phl, est, table, grad, incoming, row_out, row_in, coef_out, coef_in,
+    table_sent, table_got, grad_sent, grad_got, row_sent, row_got, coef_sent, coef_got,
+):
+    me = lax.axis_index("gz")
+    devices, rank, rows = geo.devices, geo.rank, geo.rows
+    shard = geo.pixels // devices
+    per = shard // LANES
+
+    def needs(device, owner):
+        first = geo.device_chunk(device)
+        low = lax.div(first, per)
+        high = lax.div(first + geo.win - 1, per)
+        return jnp.logical_and(low <= owner, owner <= high)
+
+    def peers(body):
+        def step(k, carry):
+            body(lax.rem(me + k, devices))
+            return carry
+
+        lax.fori_loop(1, devices, step, 0)
+
+    def table_copy(peer, owner):
+        return pltpu.make_async_remote_copy(
+            src_ref=eigen_ref,
+            dst_ref=table.at[:, columns(owner * per, per)],
+            send_sem=table_sent.at[peer],
+            recv_sem=table_got.at[owner],
+            device_id={"gz": peer},
+            device_id_type=pl.DeviceIdType.MESH,
+        )
+
+    def grad_copy(owner, source):
+        return pltpu.make_async_remote_copy(
+            src_ref=grad.at[:, columns(owner * per, per)],
+            dst_ref=incoming.at[source],
+            send_sem=grad_sent.at[owner],
+            recv_sem=grad_got.at[source],
+            device_id={"gz": owner},
+            device_id_type=pl.DeviceIdType.MESH,
+        )
+
+    def row_copy(peer, source):
+        return pltpu.make_async_remote_copy(
+            src_ref=row_out,
+            dst_ref=row_in.at[source],
+            send_sem=row_sent.at[peer],
+            recv_sem=row_got.at[source],
+            device_id={"gz": peer},
+            device_id_type=pl.DeviceIdType.MESH,
+        )
+
+    barrier = pltpu.get_barrier_semaphore()
+    peers(lambda peer: pl.semaphore_signal(
+        barrier, inc=1, device_id={"gz": peer}, device_id_type=pl.DeviceIdType.MESH
+    ))
+    pl.semaphore_wait(barrier, devices - 1)
+
+    @peers
+    def _(peer):
+        @pl.when(needs(peer, me))
+        def _():
+            table_copy(peer, me).start()
+
+    table[:, columns(me * per, per)] = eigen_ref[...]
+    grad[...] = jnp.zeros_like(grad)
+    place(geo, me, flux_ref, off_ref, word_ref, pf, pm, phl)
+
+    @peers
+    def _(peer):
+        @pl.when(needs(me, peer))
+        def _():
+            table_copy(peer, peer).wait_recv()
+
+    coef = solve(geo, me, table, pf, pm, phl, est, grad)
+
+    @peers
+    def _(peer):
+        @pl.when(needs(me, peer))
+        def _():
+            grad_copy(peer, me).start()
+
+    padded = jnp.concatenate([coef, jnp.zeros((rows, LANES - rank), jnp.float32)], axis=1)
+    lane = lax.broadcasted_iota(jnp.int32, (BS, LANES), 1)
+    row = lax.broadcasted_iota(jnp.int32, (BS, LANES), 0)
+    plan_row = lax.rem(me, half)
+    source, block = plan_ref[plan_row, 0], plan_ref[plan_row, 2]
+    group = LANES // rank
+    for h in range(BS // group):
+        here = row == lax.div(lane, rank) + h * group
+        cols = pl.ds(h * LANES, LANES)
+        sent = jnp.zeros((1, LANES), jnp.float32)
+        for b in range(NB):
+            spread = lane_take(padded[b * BS:(b + 1) * BS], lane & (rank - 1))
+            flat = jnp.sum(jnp.where(here, spread, 0.0), axis=0, keepdims=True)
+            planned = jnp.where(block == b, 1.0, 0.0)
+            gone = planned * jnp.where(source == me, 1.0, 0.0)
+            sent = sent + flat * planned
+            coef_ref[0, pl.ds(b, 1), cols] = flat * (1.0 - gone)
+        coef_out[:, cols] = sent
+    partner = lax.rem(me + half, devices)
+    coef_copy = pltpu.make_async_remote_copy(
+        src_ref=coef_out,
+        dst_ref=coef_in,
+        send_sem=coef_sent,
+        recv_sem=coef_got,
+        device_id={"gz": partner},
+        device_id_type=pl.DeviceIdType.MESH,
+    )
+    coef_copy.start()
+
+    new_ref[...] = grad[:, columns(me * per, per)]
+
+    @peers
+    def _(peer):
+        @pl.when(needs(peer, me))
+        def _():
+            grad_copy(me, peer).wait_recv()
+            new_ref[...] += incoming[peer]
+
+    update = eigen_ref[...] + geo.eta * new_ref[...]
+    new_ref[...] = update
+    squares = jnp.sum(update * update, axis=1, keepdims=True)
+    wide = lax.broadcasted_iota(jnp.int32, (rank, LANES), 1)
+    tall = lax.broadcasted_iota(jnp.int32, (rank, LANES), 0)
+    diagonal = wide == tall
+    packed = jnp.sum(jnp.where(diagonal, squares, 0.0), axis=0, keepdims=True)
+    row_out[...] = packed
+    peers(lambda peer: row_copy(peer, me).start())
+    coef_copy.wait()
+    coef_ref[0, pl.ds(NB, 1), :] = coef_in[...] * jnp.where(source == me, 0.0, 1.0)
+    row_in[me] = packed
+    peers(lambda peer: row_copy(peer, peer).wait_recv())
+    total = row_in[0]
+    for d in range(1, devices):
+        total = total + row_in[d]
+    mean = jnp.sum(jnp.where(diagonal, total, 0.0), axis=1, keepdims=True) / geo.pixels
+    new_ref[...] = new_ref[...] / jnp.sqrt(mean + 1e-06)
+
+    @peers
+    def _(peer):
+        row_copy(peer, me).wait_send()
+
+        @pl.when(needs(peer, me))
+        def _():
+            table_copy(peer, me).wait_send()
+
+        @pl.when(needs(me, peer))
+        def _():
+            grad_copy(peer, me).wait_send()
+
+
+def fused(geo, spectra, offsets, mask_bits, eigen, plan):
+    vmem = pl.BlockSpec(memory_space=pltpu.VMEM)
+    smem = pl.BlockSpec(memory_space=pltpu.SMEM)
+    shard = geo.pixels // geo.devices
+    width = BS * geo.rank
+    many = pltpu.SemaphoreType.DMA((geo.devices,))
+    one = pltpu.SemaphoreType.DMA
+    return pl.pallas_call(
+        functools.partial(fused_kernel, geo, plan.shape[0]),
+        out_shape=(
+            jax.ShapeDtypeStruct((1, NB + 1, width), jnp.float32),
+            jax.ShapeDtypeStruct((geo.rank, shard), jnp.float32),
+        ),
+        in_specs=[vmem, smem, vmem, vmem, smem],
+        out_specs=(vmem, vmem),
+        scratch_shapes=window_scratch(geo) + [
+            pltpu.VMEM((geo.rank, geo.pixels), jnp.float32),
+            pltpu.VMEM((geo.rank, geo.pixels), jnp.float32),
+            pltpu.VMEM((geo.devices, geo.rank, shard), jnp.float32),
+            pltpu.VMEM((1, LANES), jnp.float32),
+            pltpu.VMEM((geo.devices, 1, LANES), jnp.float32),
+            pltpu.VMEM((1, width), jnp.float32),
+            pltpu.VMEM((1, width), jnp.float32),
+            many, many, many, many, many, many, one, one,
+        ],
+        compiler_params=pltpu.CompilerParams(
+            vmem_limit_bytes=40 << 20, collective_id=0, has_side_effects=True
+        ),
+    )(spectra, offsets, mask_bits, eigen, plan)
+
+
 def local(spectra, offsets, mask_bits, eigen, plan):
     devices = lax.axis_size("gz")
     rank, shard = eigen.shape
     geo = Geometry(devices, spectra.shape[0], spectra.shape[1], shard * devices, rank)
+    if shard % LANES == 0:
+        return fused(geo, spectra, offsets, mask_bits, eigen, plan)
     return plain(geo, spectra, offsets, mask_bits, eigen, plan)
 
 

time: 135 us -> 35.5 us (0.26)
  blocking collectives: 55.3 us -> 0 us
  waiting for transfers between devices: 49.9 us -> 0 us
  Pallas kernels: 7.55 us -> 29.7 us
  between operations: 16.7 us -> 0.65 us
  other arithmetic: 2.45 us -> 0 us
  local copies, waits for them, and re-layouts: 2.54 us -> 4.85 us
    reduce_scatter x1 -> x0, waiting for transfers between devices: 46.8 us -> none  [plain(): mine = lax.psum_scatter(grad, 'gz', scatter_dimension=1, tiled=True)]
    psum x1 -> x0, blocking collectives: 29.6 us -> none  [plain(): squares = lax.psum(jnp.sum(update * update, axis=1), 'gz')]
    all_gather x1 -> x0, blocking collectives: 25.7 us -> none  [plain(): table = lax.all_gather(eigen, 'gz', axis=1, tiled=True)]
    pallas_call x1, Pallas kernels: 7.55 us -> 29.7 us  [fused(): pl.pallas_call(functools.partial(fused_kernel, geo, plan.shape[0]), out_s...]
    ppermute x1 -> x0, waiting for transfers between devices: 3.07 us -> none  [plain(): got = lax.ppermute(sent, 'gz', pairs)]
    unnamed x13 -> x10, local copies, waits for them, and re-layouts: 1.86 us -> 4.25 us
  transfers between devices with their start and end apart: 2 -> 0, of which waited for: 2 -> 0; matrix products, arithmetic and copies ran while one was open for 1% -> 0% of each run, Pallas kernels for 0% -> 0%
where the time goes in v2:
time: 35.5 us; the launch traced here: 35.2 us
  Pallas kernels  29.7 us (84%)
  local copies, waits for them, and re-layouts  4.85 us (14%)
  between operations  0.65 us (2%)
    pallas_call x1, Pallas kernels, fused(): pl.pallas_call(functools.partial(fused_kernel, geo, plan.shape[0]), out_s...  29.7 us
    unnamed x10, local copies, waits for them, and re-layouts  4.25 us

profile of v2, /device:TPU:0, one launch (start us, length us, event | category | flops | bytes accessed | tf_op | source)
XLA Modules:
  0.0 35.2 jit_solution(7262544229036805731)
XLA Ops:
  0.6 0.0 copy-start.3
  0.6 0.8 %copy.7.plan_ref = s32[8,3]{1,0:T(8,128)S(1)} copy(s32[8,3]{0,1:T(4,128)} %param.9) | data formatting | bytes 192 | tf_op args[4]
  1.4 0.0 copy-done.3
  1.4 0.0 copy-start
  1.4 1.2 %copy-done = f32[64,4096]{1,0:T(8,128)S(1)} copy-done((f32[64,4096]{1,0:T(8,128)S(1)}, f32[64,4096]{1,0:T(8,128)}, u32[]{:S(2)}) %copy-start) | copy-done | bytes 1048600
  2.6 0.0 copy-start.1
  2.6 0.8 %copy-done.1 = s32[64,256]{1,0:T(8,128)S(1)} copy-done((s32[64,256]{1,0:T(8,128)S(1)}, s32[64,256]{1,0:T(8,128)}, u32[]{:S(2)}) %copy-start.1) | copy-done | bytes 65560
  3.5 0.0 copy-start.2
  3.5 0.8 %copy-done.2 = f32[16,768]{1,0:T(8,128)S(1)} copy-done((f32[16,768]{1,0:T(8,128)S(1)}, f32[16,768]{1,0:T(8,128)}, u32[]{:S(2)}) %copy-start.2) | copy-done | bytes 49176
  4.3 29.7 %shard_map.68 = (f32[1,5,256]{2,1,0:T(8,128)S(1)}, f32[16,768]{1,0:T(8,128)S(1)}) custom-call(f32[64,4096]{1,0:T(8,128)S(1)} %copy-done, s32[64]{0:T(128)S(1)} %copy-done.3, s32[64,256]{1,0:T(8,128)S(1)} %copy-done.1, f32[16,768]{1,0:T(8,128)S(1)} %copy-done.2, s32[8,3]{1,0:T(8,128)S(1)} %copy.7.plan_ref), custom_call_target="tpu_custom_call" | custom-call | tf_op jit(solution)/shard_map/pallas_call | solution.py:375
  34.0 0.6 %copy.8 = f32[1,5,256]{2,0,1:T(1,128)} copy(f32[1,5,256]{2,1,0:T(8,128)S(1)} %get-tuple-element.2) | data formatting | bytes 10240 | tf_op jit(solution)/shard_map/pallas_call | solution.py:375
  34.6 0.6 %copy.10 = f32[16,768]{1,0:T(8,128)} copy(f32[16,768]{1,0:T(8,128)S(1)} %get-tuple-element.7) | data formatting | bytes 98304
Async XLA Ops:
  0.6 0.8 %copy-start.3 = (s32[64]{0:T(128)S(1)}, s32[64]{0:T(128)}, u32[]{:S(2)}) copy-start(s32[64]{0:T(128)} %off_ref.1) | copy-start | bytes 772
  1.4 1.2 %copy-start = (f32[64,4096]{1,0:T(8,128)S(1)}, f32[64,4096]{1,0:T(8,128)}, u32[]{:S(2)}) copy-start(f32[64,4096]{1,0:T(8,128)} %flux_ref.1) | copy-start | bytes 3145732
  2.6 0.8 %copy-start.1 = (s32[64,256]{1,0:T(8,128)S(1)}, s32[64,256]{1,0:T(8,128)}, u32[]{:S(2)}) copy-start(s32[64,256]{1,0:T(8,128)} %word_ref.1) | copy-start | bytes 196612
  3.5 0.8 %copy-start.2 = (f32[16,768]{1,0:T(8,128)S(1)}, f32[16,768]{1,0:T(8,128)}, u32[]{:S(2)}) copy-start(f32[16,768]{1,0:T(8,128)} %eigen_ref.1) | copy-start | bytes 147460

commit v3 on v2

--- a/solution.py
+++ b/solution.py
@@ -34,6 +34,22 @@
     def aligned(self, spectrum, chunks):
         start = lax.div(lax.div(spectrum * self.ramp, self.total), LANES)
         return jnp.minimum(start, self.pixels // LANES - chunks)
+
+    def static_range(self, device):
+        first = min(device * self.rows * self.ramp // self.total // LANES,
+                    self.pixels // LANES - self.win)
+        per = self.pixels // self.devices // LANES
+        return first // per, (first + self.win - 1) // per
+
+    def ranges(self, me):
+        shards = [self.static_range(d) for d in range(self.devices)]
+        low, high, first, last = 0, 0, 0, -1
+        for d, (a, b) in enumerate(shards):
+            low = jnp.where(me == d, a, low)
+            high = jnp.where(me == d, b, high)
+            first = first + jnp.where(me > b, 1, 0)
+            last = last + jnp.where(me >= a, 1, 0)
+        return low, high, first, last
 
     def device_chunk(self, device):
         return self.aligned(device * self.rows, self.win)
@@ -123,7 +139,7 @@
     lax.fori_loop(0, NB, body, 0)
 
 
-def solve(geo, me, table, pf, pm, phl, est, grad):
+def solve(geo, me, table, pf, pm, phl, est, grad, after=None):
     rank, rows = geo.rank, geo.rows
     start = geo.device_chunk(me)
     step = TILE // LANES
@@ -159,6 +175,8 @@
         grad[:, columns(start + t * step, step)] = jnp.dot(
             across, stack, preferred_element_type=jnp.float32
         )
+        if after is not None and (t + 1 == tiles or t % 5 == 4):
+            after(start + (t + 1) * step, t + 1 == tiles)
     return coef
 
 
@@ -213,20 +231,16 @@
 
 
 def fused_kernel(
-    geo, half, flux_ref, off_ref, word_ref, eigen_ref, plan_ref, coef_ref, new_ref,
-    pf, pm, phl, est, table, grad, incoming, row_out, row_in, coef_out, coef_in,
+    geo, half, flux_hbm, off_ref, word_hbm, eigen_hbm, plan_ref, coef_ref, new_ref,
+    pf, pm, phl, est, flux_ref, word_ref, table, grad, incoming,
+    row_out, row_in, coef_out, coef_in, local_done,
     table_sent, table_got, grad_sent, grad_got, row_sent, row_got, coef_sent, coef_got,
 ):
     me = lax.axis_index("gz")
     devices, rank, rows = geo.devices, geo.rank, geo.rows
     shard = geo.pixels // devices
     per = shard // LANES
-
-    def needs(device, owner):
-        first = geo.device_chunk(device)
-        low = lax.div(first, per)
-        high = lax.div(first + geo.win - 1, per)
-        return jnp.logical_and(low <= owner, owner <= high)
+    low, high, first, last = geo.ranges(me)
 
     def peers(body):
         def step(k, carry):
@@ -235,9 +249,19 @@
 
         lax.fori_loop(1, devices, step, 0)
 
+    def others(start, stop, body):
+        def step(k, carry):
+            @pl.when(k != me)
+            def _():
+                body(k)
+
+            return carry
+
+        lax.fori_loop(start, stop, step, 0)
+
     def table_copy(peer, owner):
         return pltpu.make_async_remote_copy(
-            src_ref=eigen_ref,
+            src_ref=eigen_hbm,
             dst_ref=table.at[:, columns(owner * per, per)],
             send_sem=table_sent.at[peer],
             recv_sem=table_got.at[owner],
@@ -265,41 +289,39 @@
             device_id_type=pl.DeviceIdType.MESH,
         )
 
+    copies = [
+        pltpu.make_async_copy(flux_hbm, flux_ref, local_done.at[0]),
+        pltpu.make_async_copy(word_hbm, word_ref, local_done.at[1]),
+        pltpu.make_async_copy(eigen_hbm, table.at[:, columns(me * per, per)], local_done.at[2]),
+    ]
+    for copy in copies:
+        copy.start()
     barrier = pltpu.get_barrier_semaphore()
     peers(lambda peer: pl.semaphore_signal(
         barrier, inc=1, device_id={"gz": peer}, device_id_type=pl.DeviceIdType.MESH
     ))
     pl.semaphore_wait(barrier, devices - 1)
-
-    @peers
-    def _(peer):
-        @pl.when(needs(peer, me))
-        def _():
-            table_copy(peer, me).start()
-
-    table[:, columns(me * per, per)] = eigen_ref[...]
+    others(first, last + 1, lambda peer: table_copy(peer, me).start())
     grad[...] = jnp.zeros_like(grad)
+    copies[0].wait()
+    copies[1].wait()
     place(geo, me, flux_ref, off_ref, word_ref, pf, pm, phl)
-
-    @peers
-    def _(peer):
-        @pl.when(needs(me, peer))
-        def _():
-            table_copy(peer, peer).wait_recv()
-
-    coef = solve(geo, me, table, pf, pm, phl, est, grad)
-
-    @peers
-    def _(peer):
-        @pl.when(needs(me, peer))
-        def _():
-            grad_copy(peer, me).start()
+    copies[2].wait()
+    others(low, high + 1, lambda owner: table_copy(owner, owner).wait_recv())
+    begun = [low]
+
+    def after(chunk, done):
+        stop = high + 1 if done else lax.div(chunk, per)
+        others(begun[0], stop, lambda owner: grad_copy(owner, me).start())
+        begun[0] = stop
+
+    coef = solve(geo, me, table, pf, pm, phl, est, grad, after)
 
     padded = jnp.concatenate([coef, jnp.zeros((rows, LANES - rank), jnp.float32)], axis=1)
     lane = lax.broadcasted_iota(jnp.int32, (BS, LANES), 1)
     row = lax.broadcasted_iota(jnp.int32, (BS, LANES), 0)
     plan_row = lax.rem(me, half)
-    source, block = plan_ref[plan_row, 0], plan_ref[plan_row, 2]
+    source, block = plan_ref[0, plan_row], plan_ref[2, plan_row]
     group = LANES // rank
     for h in range(BS // group):
         here = row == lax.div(lane, rank) + h * group
@@ -326,14 +348,12 @@
 
     new_ref[...] = grad[:, columns(me * per, per)]
 
-    @peers
-    def _(peer):
-        @pl.when(needs(peer, me))
-        def _():
-            grad_copy(me, peer).wait_recv()
-            new_ref[...] += incoming[peer]
-
-    update = eigen_ref[...] + geo.eta * new_ref[...]
+    def add(peer):
+        grad_copy(me, peer).wait_recv()
+        new_ref[...] += incoming[peer]
+
+    others(first, last + 1, add)
+    update = table[:, columns(me * per, per)] + geo.eta * new_ref[...]
     new_ref[...] = update
     squares = jnp.sum(update * update, axis=1, keepdims=True)
     wide = lax.broadcasted_iota(jnp.int32, (rank, LANES), 1)
@@ -352,22 +372,15 @@
     mean = jnp.sum(jnp.where(diagonal, total, 0.0), axis=1, keepdims=True) / geo.pixels
     new_ref[...] = new_ref[...] / jnp.sqrt(mean + 1e-06)
 
-    @peers
-    def _(peer):
-        row_copy(peer, me).wait_send()
-
-        @pl.when(needs(peer, me))
-        def _():
-            table_copy(peer, me).wait_send()
-
-        @pl.when(needs(me, peer))
-        def _():
-            grad_copy(peer, me).wait_send()
+    peers(lambda peer: row_copy(peer, me).wait_send())
+    others(first, last + 1, lambda peer: table_copy(peer, me).wait_send())
+    others(low, high + 1, lambda owner: grad_copy(owner, me).wait_send())
 
 
 def fused(geo, spectra, offsets, mask_bits, eigen, plan):
     vmem = pl.BlockSpec(memory_space=pltpu.VMEM)
     smem = pl.BlockSpec(memory_space=pltpu.SMEM)
+    hbm = pl.BlockSpec(memory_space=pltpu.HBM)
     shard = geo.pixels // geo.devices
     width = BS * geo.rank
     many = pltpu.SemaphoreType.DMA((geo.devices,))
@@ -378,9 +391,11 @@
             jax.ShapeDtypeStruct((1, NB + 1, width), jnp.float32),
             jax.ShapeDtypeStruct((geo.rank, shard), jnp.float32),
         ),
-        in_specs=[vmem, smem, vmem, vmem, smem],
+        in_specs=[hbm, smem, hbm, hbm, smem],
         out_specs=(vmem, vmem),
         scratch_shapes=window_scratch(geo) + [
+            pltpu.VMEM(spectra.shape, jnp.float32),
+            pltpu.VMEM(mask_bits.shape, jnp.int32),
             pltpu.VMEM((geo.rank, geo.pixels), jnp.float32),
             pltpu.VMEM((geo.rank, geo.pixels), jnp.float32),
             pltpu.VMEM((geo.devices, geo.rank, shard), jnp.float32),
@@ -388,12 +403,13 @@
             pltpu.VMEM((geo.devices, 1, LANES), jnp.float32),
             pltpu.VMEM((1, width), jnp.float32),
             pltpu.VMEM((1, width), jnp.float32),
+            pltpu.SemaphoreType.DMA((3,)),
             many, many, many, many, many, many, one, one,
         ],
         compiler_params=pltpu.CompilerParams(
-            vmem_limit_bytes=40 << 20, collective_id=0, has_side_effects=True
+            vmem_limit_bytes=64 << 20, collective_id=0, has_side_effects=True
         ),
-    )(spectra, offsets, mask_bits, eigen, plan)
+    )(spectra, offsets, mask_bits, eigen, plan.T)
 
 
 def local(spectra, offsets, mask_bits, eigen, plan):

time: 35.5 us -> 32.9 us (0.927)
  local copies, waits for them, and re-layouts: 4.85 us -> 2.72 us
  Pallas kernels: 29.7 us -> 29.3 us
    unnamed x10 -> x1, local copies, waits for them, and re-layouts: 4.25 us -> 1.42 us
    pallas_call x1, local copies, waits for them, and re-layouts: 0.6 us -> 1.3 us  [fused(): pl.pallas_call(functools.partial(fused_kernel, geo, plan.shape[0]), out_s...]
    pallas_call x1, Pallas kernels: 29.7 us -> 29.3 us  [fused(): pl.pallas_call(functools.partial(fused_kernel, geo, plan.shape[0]), out_s...]
where the time goes in v3:
time: 32.9 us; the launch traced here: 32.7 us
  Pallas kernels  29.3 us (89%)
  local copies, waits for them, and re-layouts  2.72 us (8%)
  between operations  0.64 us (2%)
    pallas_call x1, Pallas kernels, fused(): pl.pallas_call(functools.partial(fused_kernel, geo, plan.shape[0]), out_s...  29.3 us
    unnamed x1, local copies, waits for them, and re-layouts  1.42 us
    pallas_call x1, local copies, waits for them, and re-layouts, fused(): pl.pallas_call(functools.partial(fused_kernel, geo, plan.shape[0]), out_s...  1.3 us

profile of v3, /device:TPU:0, one launch (start us, length us, event | category | flops | bytes accessed | tf_op | source)
XLA Modules:
  0.0 32.7 jit_solution(9031341731632469789)
XLA Ops:
  0.6 29.3 %shard_map.68 = (f32[1,5,256]{2,1,0:T(8,128)}, f32[16,768]{1,0:T(8,128)}) custom-call(f32[64,4096]{1,0:T(8,128)} %flux_hbm.1, s32[64]{0:T(128)} %off_ref.1, s32[64,256]{1,0:T(8,128)} %word_hbm.1, f32[16,768]{1,0:T(8,128)} %eigen_hbm.1, s32[3,8]{1,0:T(4,128)} %bitcast.1), custom_call_target="tpu_custom_call" | custom-call | tf_op jit(solution)/shard_map/pallas_call | solution.py:388
  30.0 1.3 %copy.7 = f32[1,5,256]{2,0,1:T(1,128)} copy(f32[1,5,256]{2,1,0:T(8,128)} %get-tuple-element.2) | data formatting | bytes 10240 | tf_op jit(solution)/shard_map/pallas_call | solution.py:388
  31.3 1.4 %copy.9 = f32[16,768]{1,0:T(8,128)} copy(f32[16,768]{1,0:T(8,128)} %get-tuple-element.7) | data formatting | bytes 98304

commit v4 on v3

--- a/solution.py
+++ b/solution.py
@@ -139,20 +139,21 @@
     lax.fori_loop(0, NB, body, 0)
 
 
-def solve(geo, me, table, pf, pm, phl, est, grad, after=None):
+def split_table(rank, table, est, cols):
+    high, low = split(table[:, cols])
+    est[pl.ds(0, rank), cols] = high
+    est[pl.ds(rank, rank), cols] = low
+    est[pl.ds(2 * rank, rank), cols] = high
+
+
+def solve(geo, me, pf, pm, phl, est, grad, after=None):
     rank, rows = geo.rank, geo.rows
     start = geo.device_chunk(me)
     step = TILE // LANES
     tiles = geo.win // step
-    for t in range(tiles):
-        high, low = split(table[:, columns(start + t * step, step)])
-        cols = pl.ds(t * TILE, TILE)
-        est[pl.ds(0, rank), cols] = high
-        est[pl.ds(rank, rank), cols] = low
-        est[pl.ds(2 * rank, rank), cols] = high
     both = lax.dot_general(
         phl[...],
-        est[pl.ds(0, 2 * rank), :],
+        est[pl.ds(0, 2 * rank), columns(start, geo.win)],
         (((1,), (1,)), ((), ())),
         preferred_element_type=jnp.float32,
     )
@@ -167,7 +168,8 @@
     across = jnp.concatenate([high, high, low], axis=1).astype(jnp.bfloat16)
     for t in range(tiles):
         cols = pl.ds(t * TILE, TILE)
-        fit = jnp.dot(left, est[:, cols], preferred_element_type=jnp.float32)
+        band = est[:, columns(start + t * step, step)]
+        fit = jnp.dot(left, band, preferred_element_type=jnp.float32)
         resid = pf[:, cols] - pm[:, cols] * fit
         weighted = resid / (1.0 + resid * resid)
         high, low = split(weighted)
@@ -184,7 +186,11 @@
     me = lax.axis_index("gz")
     grad_ref[...] = jnp.zeros_like(grad_ref)
     place(geo, me, flux_ref, off_ref, word_ref, pf, pm, phl)
-    coef_ref[...] = solve(geo, me, table_ref, pf, pm, phl, est, grad_ref)
+    start = geo.device_chunk(me)
+    for t in range(geo.win * LANES // TILE):
+        cols = columns(start + t * (TILE // LANES), TILE // LANES)
+        split_table(geo.rank, table_ref, est, cols)
+    coef_ref[...] = solve(geo, me, pf, pm, phl, est, grad_ref)
 
 
 def window_scratch(geo):
@@ -192,7 +198,7 @@
         pltpu.VMEM((geo.rows, geo.window), jnp.float32),
         pltpu.VMEM((geo.rows, geo.window), jnp.float32),
         pltpu.VMEM((2 * geo.rows, geo.window), jnp.bfloat16),
-        pltpu.VMEM((3 * geo.rank, geo.window), jnp.bfloat16),
+        pltpu.VMEM((3 * geo.rank, geo.pixels), jnp.bfloat16),
     ]
 
 
@@ -301,13 +307,35 @@
         barrier, inc=1, device_id={"gz": peer}, device_id_type=pl.DeviceIdType.MESH
     ))
     pl.semaphore_wait(barrier, devices - 1)
-    others(first, last + 1, lambda peer: table_copy(peer, me).start())
+    def send(i, carry):
+        half_way = lax.div(i, 2)
+        peer = jnp.where(lax.rem(i, 2) == 0, first + half_way, last - half_way)
+
+        @pl.when(peer != me)
+        def _():
+            table_copy(peer, me).start()
+
+        return carry
+
+    lax.fori_loop(0, last - first + 1, send, 0)
     grad[...] = jnp.zeros_like(grad)
     copies[0].wait()
     copies[1].wait()
     place(geo, me, flux_ref, off_ref, word_ref, pf, pm, phl)
     copies[2].wait()
-    others(low, high + 1, lambda owner: table_copy(owner, owner).wait_recv())
+
+    def receive(i, carry):
+        turn = me + i
+        owner = jnp.where(turn > high, turn - (high + 1 - low), turn)
+
+        @pl.when(owner != me)
+        def _():
+            table_copy(owner, owner).wait_recv()
+
+        split_table(rank, table, est, columns(owner * per, per))
+        return carry
+
+    lax.fori_loop(0, high + 1 - low, receive, 0)
     begun = [low]
 
     def after(chunk, done):
@@ -315,7 +343,7 @@
         others(begun[0], stop, lambda owner: grad_copy(owner, me).start())
         begun[0] = stop
 
-    coef = solve(geo, me, table, pf, pm, phl, est, grad, after)
+    coef = solve(geo, me, pf, pm, phl, est, grad, after)
 
     padded = jnp.concatenate([coef, jnp.zeros((rows, LANES - rank), jnp.float32)], axis=1)
     lane = lax.broadcasted_iota(jnp.int32, (BS, LANES), 1)

time: 32.9 us -> 33 us (level)
  no operation moved by 1% of the time
where the time goes in v4:
time: 33 us; the launch traced here: 32.8 us
  Pallas kernels  29.4 us (89%)
  local copies, waits for them, and re-layouts  2.72 us (8%)
  between operations  0.64 us (2%)
    pallas_call x1, Pallas kernels, fused(): pl.pallas_call(functools.partial(fused_kernel, geo, plan.shape[0]), out_s...  29.4 us
    unnamed x1, local copies, waits for them, and re-layouts  1.42 us
    pallas_call x1, local copies, waits for them, and re-layouts, fused(): pl.pallas_call(functools.partial(fused_kernel, geo, plan.shape[0]), out_s...  1.3 us

profile of v4, /device:TPU:0, one launch (start us, length us, event | category | flops | bytes accessed | tf_op | source)
XLA Modules:
  0.0 32.8 jit_solution(3369752695971211425)
XLA Ops:
  0.6 29.4 %shard_map.68 = (f32[1,5,256]{2,1,0:T(8,128)}, f32[16,768]{1,0:T(8,128)}) custom-call(f32[64,4096]{1,0:T(8,128)} %flux_hbm.1, s32[64]{0:T(128)} %off_ref.1, s32[64,256]{1,0:T(8,128)} %word_hbm.1, f32[16,768]{1,0:T(8,128)} %eigen_hbm.1, s32[3,8]{1,0:T(4,128)} %bitcast.1), custom_call_target="tpu_custom_call" | custom-call | tf_op jit(solution)/shard_map/pallas_call | solution.py:416
  30.1 1.3 %copy.7 = f32[1,5,256]{2,0,1:T(1,128)} copy(f32[1,5,256]{2,1,0:T(8,128)} %get-tuple-element.2) | data formatting | bytes 10240 | tf_op jit(solution)/shard_map/pallas_call | solution.py:416
  31.4 1.4 %copy.9 = f32[16,768]{1,0:T(8,128)} copy(f32[16,768]{1,0:T(8,128)} %get-tuple-element.7) | data formatting | bytes 98304

commit v5 on v4

--- a/solution.py
+++ b/solution.py
@@ -13,6 +13,7 @@
 SPAN = 128
 LANES = 128
 TILE = 256
+GROUP = 4
 
 
 class Geometry:
@@ -239,7 +240,7 @@
 def fused_kernel(
     geo, half, flux_hbm, off_ref, word_hbm, eigen_hbm, plan_ref, coef_ref, new_ref,
     pf, pm, phl, est, flux_ref, word_ref, table, grad, incoming,
-    row_out, row_in, coef_out, coef_in, local_done,
+    row_out, row_mid, row_in, coef_out, coef_in, local_done,
     table_sent, table_got, grad_sent, grad_got, row_sent, row_got, coef_sent, coef_got,
 ):
     me = lax.axis_index("gz")
@@ -285,9 +286,9 @@
             device_id_type=pl.DeviceIdType.MESH,
         )
 
-    def row_copy(peer, source):
+    def row_copy(peer, source, row_from):
         return pltpu.make_async_remote_copy(
-            src_ref=row_out,
+            src_ref=row_from,
             dst_ref=row_in.at[source],
             send_sem=row_sent.at[peer],
             recv_sem=row_got.at[source],
@@ -389,18 +390,37 @@
     diagonal = wide == tall
     packed = jnp.sum(jnp.where(diagonal, squares, 0.0), axis=0, keepdims=True)
     row_out[...] = packed
-    peers(lambda peer: row_copy(peer, me).start())
+    team = GROUP if devices % GROUP == 0 else devices
+    base = lax.div(me, team) * team
+    place_in = lax.rem(me, team)
+    near = [base + lax.rem(place_in + k, team) for k in range(1, team)]
+    far = [lax.rem(me + k * team, devices) for k in range(1, devices // team)]
+    row_in[me] = packed
+    for peer in near:
+        row_copy(peer, me, row_out).start()
     coef_copy.wait()
     coef_ref[0, pl.ds(NB, 1), :] = coef_in[...] * jnp.where(source == me, 0.0, 1.0)
-    row_in[me] = packed
-    peers(lambda peer: row_copy(peer, peer).wait_recv())
-    total = row_in[0]
-    for d in range(1, devices):
-        total = total + row_in[d]
+    for peer in near:
+        row_copy(peer, peer, row_out).wait_recv()
+    total = row_in[base]
+    for d in range(1, team):
+        total = total + row_in[base + d]
+    row_mid[...] = total
+    for peer in far:
+        row_copy(peer, me, row_mid).start()
+    row_in[me] = total
+    for peer in far:
+        row_copy(peer, peer, row_mid).wait_recv()
+    total = row_in[place_in]
+    for d in range(1, devices // team):
+        total = total + row_in[place_in + d * team]
     mean = jnp.sum(jnp.where(diagonal, total, 0.0), axis=1, keepdims=True) / geo.pixels
     new_ref[...] = new_ref[...] / jnp.sqrt(mean + 1e-06)
 
-    peers(lambda peer: row_copy(peer, me).wait_send())
+    for peer in near:
+        row_copy(peer, me, row_out).wait_send()
+    for peer in far:
+        row_copy(peer, me, row_mid).wait_send()
     others(first, last + 1, lambda peer: table_copy(peer, me).wait_send())
     others(low, high + 1, lambda owner: grad_copy(owner, me).wait_send())
 
@@ -428,6 +448,7 @@
             pltpu.VMEM((geo.rank, geo.pixels), jnp.float32),
             pltpu.VMEM((geo.devices, geo.rank, shard), jnp.float32),
             pltpu.VMEM((1, LANES), jnp.float32),
+            pltpu.VMEM((1, LANES), jnp.float32),
             pltpu.VMEM((geo.devices, 1, LANES), jnp.float32),
             pltpu.VMEM((1, width), jnp.float32),
             pltpu.VMEM((1, width), jnp.float32),

time: 33 us -> 33.4 us (1.012)
  Pallas kernels: 29.4 us -> 29.8 us
    pallas_call x1, Pallas kernels: 29.4 us -> 29.8 us  [fused(): pl.pallas_call(functools.partial(fused_kernel, geo, plan.shape[0]), out_s...]
where the time goes in v5:
time: 33.4 us; the launch traced here: 33.2 us
  Pallas kernels  29.8 us (89%)
  local copies, waits for them, and re-layouts  2.72 us (8%)
  between operations  0.64 us (2%)
    pallas_call x1, Pallas kernels, fused(): pl.pallas_call(functools.partial(fused_kernel, geo, plan.shape[0]), out_s...  29.8 us
    unnamed x1, local copies, waits for them, and re-layouts  1.42 us
    pallas_call x1, local copies, waits for them, and re-layouts, fused(): pl.pallas_call(functools.partial(fused_kernel, geo, plan.shape[0]), out_s...  1.3 us

profile of v5, /device:TPU:0, one launch (start us, length us, event | category | flops | bytes accessed | tf_op | source)
XLA Modules:
  0.0 33.2 jit_solution(12560917628893737032)
XLA Ops:
  0.6 29.8 %shard_map.68 = (f32[1,5,256]{2,1,0:T(8,128)}, f32[16,768]{1,0:T(8,128)}) custom-call(f32[64,4096]{1,0:T(8,128)} %flux_hbm.1, s32[64]{0:T(128)} %off_ref.1, s32[64,256]{1,0:T(8,128)} %word_hbm.1, f32[16,768]{1,0:T(8,128)} %eigen_hbm.1, s32[3,8]{1,0:T(4,128)} %bitcast.1), custom_call_target="tpu_custom_call" | custom-call | tf_op jit(solution)/shard_map/pallas_call | solution.py:436
  30.4 1.3 %copy.7 = f32[1,5,256]{2,0,1:T(1,128)} copy(f32[1,5,256]{2,1,0:T(8,128)} %get-tuple-element.2) | data formatting | bytes 10240 | tf_op jit(solution)/shard_map/pallas_call | solution.py:436
  31.7 1.4 %copy.9 = f32[16,768]{1,0:T(8,128)} copy(f32[16,768]{1,0:T(8,128)} %get-tuple-element.7) | data formatting | bytes 98304

commit v6 on v4

--- a/solution.py
+++ b/solution.py
@@ -435,7 +435,7 @@
             many, many, many, many, many, many, one, one,
         ],
         compiler_params=pltpu.CompilerParams(
-            vmem_limit_bytes=64 << 20, collective_id=0, has_side_effects=True
+            vmem_limit_bytes=53 << 20, collective_id=0, has_side_effects=True
         ),
     )(spectra, offsets, mask_bits, eigen, plan.T)
 

time: 33 us -> 33.7 us (1.021)
  local copies, waits for them, and re-layouts: 2.72 us -> 4.19 us
  Pallas kernels: 29.4 us -> 28.6 us
    unnamed x1 -> x9, local copies, waits for them, and re-layouts: 1.42 us -> 3.59 us
    pallas_call x1, Pallas kernels: 29.4 us -> 28.6 us  [fused(): pl.pallas_call(functools.partial(fused_kernel, geo, plan.shape[0]), out_s...]
    pallas_call x1, local copies, waits for them, and re-layouts: 1.3 us -> 0.6 us  [fused(): pl.pallas_call(functools.partial(fused_kernel, geo, plan.shape[0]), out_s...]
where the time goes in v6:
time: 33.7 us; the launch traced here: 33.4 us
  Pallas kernels  28.6 us (85%)
  local copies, waits for them, and re-layouts  4.19 us (12%)
  between operations  0.65 us (2%)
    pallas_call x1, Pallas kernels, fused(): pl.pallas_call(functools.partial(fused_kernel, geo, plan.shape[0]), out_s...  28.6 us
    unnamed x9, local copies, waits for them, and re-layouts  3.59 us

profile of v6, /device:TPU:0, one launch (start us, length us, event | category | flops | bytes accessed | tf_op | source)
XLA Modules:
  0.0 33.4 jit_solution(15461872691268717385)
XLA Ops:
  0.6 0.0 copy-start.3
  0.6 0.6 %copy-done.3 = s32[64]{0:T(128)S(1)} copy-done((s32[64]{0:T(128)S(1)}, s32[64]{0:T(128)}, u32[]{:S(2)}) %copy-start.3) | copy-done | bytes 280
  1.3 0.0 copy-start
  1.3 0.8 %copy-done = s32[64,256]{1,0:T(8,128)S(1)} copy-done((s32[64,256]{1,0:T(8,128)S(1)}, s32[64,256]{1,0:T(8,128)}, u32[]{:S(2)}) %copy-start) | copy-done | bytes 65560
  2.1 0.0 copy-start.1
  2.1 0.8 %copy-done.1 = f32[16,768]{1,0:T(8,128)S(1)} copy-done((f32[16,768]{1,0:T(8,128)S(1)}, f32[16,768]{1,0:T(8,128)}, u32[]{:S(2)}) %copy-start.1) | copy-done | bytes 49176
  2.9 0.0 copy-start.2
  2.9 0.7 %copy-done.2 = s32[8,3]{0,1:T(4,128)S(1)} copy-done((s32[8,3]{0,1:T(4,128)S(1)}, s32[8,3]{0,1:T(4,128)}, u32[]{:S(2)}) %copy-start.2) | copy-done | bytes 120
  3.6 28.6 %shard_map.68 = (f32[1,5,256]{2,1,0:T(8,128)S(1)}, f32[16,768]{1,0:T(8,128)S(1)}) custom-call(f32[64,4096]{1,0:T(8,128)} %flux_hbm.1, s32[64]{0:T(128)S(1)} %copy-done.3, s32[64,256]{1,0:T(8,128)S(1)} %copy-done, f32[16,768]{1,0:T(8,128)S(1)} %copy-done.1, s32[3,8]{1,0:T(4,128)S(1)} %bitcast.1), custom_call_target="tpu_custom_call" | custom-call | tf_op jit(solution)/shard_map/pallas_call | solution.py:416
  32.2 0.6 %copy.7 = f32[1,5,256]{2,0,1:T(1,128)} copy(f32[1,5,256]{2,1,0:T(8,128)S(1)} %get-tuple-element.2) | data formatting | bytes 10240 | tf_op jit(solution)/shard_map/pallas_call | solution.py:416
  32.8 0.6 %copy.9 = f32[16,768]{1,0:T(8,128)} copy(f32[16,768]{1,0:T(8,128)S(1)} %get-tuple-element.7) | data formatting | bytes 98304
Async XLA Ops:
  0.6 0.7 %copy-start.3 = (s32[64]{0:T(128)S(1)}, s32[64]{0:T(128)}, u32[]{:S(2)}) copy-start(s32[64]{0:T(128)} %off_ref.1) | copy-start | bytes 772
  1.3 0.8 %copy-start = (s32[64,256]{1,0:T(8,128)S(1)}, s32[64,256]{1,0:T(8,128)}, u32[]{:S(2)}) copy-start(s32[64,256]{1,0:T(8,128)} %word_hbm.1) | copy-start | bytes 196612
  2.1 0.8 %copy-start.1 = (f32[16,768]{1,0:T(8,128)S(1)}, f32[16,768]{1,0:T(8,128)}, u32[]{:S(2)}) copy-start(f32[16,768]{1,0:T(8,128)} %eigen_hbm.1) | copy-start | bytes 147460
  2.9 0.7 %copy-start.2 = (s32[8,3]{0,1:T(4,128)S(1)}, s32[8,3]{0,1:T(4,128)}, u32[]{:S(2)}) copy-start(s32[8,3]{0,1:T(4,128)} %param.9) | copy-start | bytes 292
